TPU v7x, 32 devices: a whole 2x2x4 slice. The times are simulated.
32 devices in a mesh: groups: 2 (over x), seq: 16 (over z, y, core).
Axes of the slice: x: 2, y: 2, z: 4, core: 2. Of those that a mesh axis runs over, the one named last changes fastest.
Arguments:
- queries: bfloat16 [4096, 4096], P(('groups', 'seq')), parts along dimension 0, may hold values from -200 to 200
- response_keys: bfloat16 [4096, 512], P(('groups', 'seq')), parts along dimension 0, may hold values from -6 to 6
- response_values: bfloat16 [4096, 512], P(('groups', 'seq')), parts along dimension 0, may hold values from -6 to 6
- prompt_key_rows: bfloat16 [8192, 512], P(('groups', 'seq')), parts along dimension 0, may hold values from -6 to 6
- prompt_value_rows: bfloat16 [8192, 512], P(('groups', 'seq')), parts along dimension 0, may hold values from -6 to 6
- upstream: bfloat16 [4096, 4096], P(('groups', 'seq')), parts along dimension 0, may hold values from -6 to 6
- prompt_len: int32 [8], P('groups'), parts along dimension 0, may hold values from 256 to 1024, as said below
- prompt_owner: int32 [8], P('groups'), parts along dimension 0, may hold values from 0 to 3, as said below
- response_prompt: int32 [64], P(('groups', 'seq')), parts along dimension 0, may hold values from 0 to 3, as said below
- response_len: int32 [64], P(('groups', 'seq')), parts along dimension 0, may hold values from 1 to 64, as said below
Outputs:
- attn_out: bfloat16 [4096, 4096], P(('groups', 'seq')), parts along dimension 0
- grad_queries: bfloat16 [4096, 4096], P(('groups', 'seq')), parts along dimension 0
- grad_resp_keys: bfloat16 [4096, 512], P(('groups', 'seq')), parts along dimension 0
- grad_resp_values: bfloat16 [4096, 512], P(('groups', 'seq')), parts along dimension 0
- grad_prefix_keys: float32 [8192, 512], P(('groups', 'seq')), parts along dimension 0
- grad_prefix_values: float32 [8192, 512], P(('groups', 'seq')), parts along dimension 0
There are 2 independent parts, one for each index of `groups`. A program takes and returns all parts, laid end to end along the dimension named above; each array names one. Nothing has to cross between parts.
Inputs may be any that keep to these rules, and one draw needn't show every extreme that they name: `prompt_len`: some prompt has exactly 1024 tokens. `prompt_owner`: A permutation of the blocks; block b is the devices b * 4 to (b + 1) * 4 - 1, which hold prefix rows b * 1024 to (b + 1) * 1024 - 1. `response_prompt`: the 8 slots of block c (slots c * 8 to (c + 1) * 8 - 1) all hold responses of one prompt, owned by block c or by block c xor 1; blocks c and c xor 1 either both hold their own prompts or hold each other's. So each prompt has 8 responses. `response_len`: some response has exactly 64 tokens.
All inputs are finite; a program needn't handle non-finite values.
Results may differ from a plain program's by a relative error of at most 0.005.
Values may be sent and summed in bfloat16 or wider, within the bound.
A program may use at most 64 MiB of HBM per device.

v0:
```python
import math

import jax
import jax.numpy as jnp
from jax import lax
from jax.sharding import PartitionSpec as P

QUERY_HEADS = 32
KEY_VALUE_HEADS = 4
HEAD_WIDTH = 128
GROUP_RESPONSES = 8
SLOTS = 2
RESPONSE_LENGTH = 64
PROMPT_MAXIMUM = 1024


def swapped(block, axis, apart):
    count = lax.axis_size(axis)
    route = []
    for low in range(count):
        high = low | 1 << apart
        if high != low and high < count:
            route += [(low, high), (high, low)]
    return lax.ppermute(block, axis, route)


def attend_head(
    query_block,
    grad_block,
    own_response_keys,
    own_response_values,
    common_keys,
    common_values,
    pre_len,
    resp_len,
):
    score_scale = 1.0 / math.sqrt(HEAD_WIDTH)
    exact = jnp.float32
    positions = jnp.arange(RESPONSE_LENGTH, dtype=jnp.int32)
    live_rows = positions[None, :] < resp_len[:, None]
    shared_mask = jnp.arange(PROMPT_MAXIMUM, dtype=jnp.int32) < pre_len
    self_mask = (positions[None, None, :] <= positions[None, :, None]) & (
        positions[None, None, :] < resp_len[:, None, None]
    )
    shared_scores = (
        jnp.einsum("slrd,pd->srlp", query_block, common_keys, preferred_element_type=exact)
        * score_scale
    )
    self_scores = (
        jnp.einsum("sird,sjd->srij", query_block, own_response_keys, preferred_element_type=exact)
        * score_scale
    )
    shared_scores = jnp.where(shared_mask[None, None, None, :], shared_scores, -jnp.inf)
    self_scores = jnp.where(self_mask[:, None, :, :], self_scores, -jnp.inf)
    row_max = jnp.maximum(jnp.max(shared_scores, axis=-1), jnp.max(self_scores, axis=-1))
    shared_exp = jnp.exp(shared_scores - row_max[..., None])
    self_exp = jnp.exp(self_scores - row_max[..., None])
    row_total = jnp.sum(shared_exp, axis=-1) + jnp.sum(self_exp, axis=-1)
    shared_prob = shared_exp / row_total[..., None]
    self_prob = self_exp / row_total[..., None]
    shared_weight = shared_prob.astype(jnp.bfloat16)
    self_weight = self_prob.astype(jnp.bfloat16)
    blended_output = jnp.einsum(
        "srlp,pd->slrd", shared_weight, common_values, preferred_element_type=exact
    )
    blended_output = blended_output + jnp.einsum(
        "srij,sjd->sird", self_weight, own_response_values, preferred_element_type=exact
    )
    live_four = live_rows[:, :, None, None]
    blended_output = jnp.where(live_four, blended_output, 0.0)
    grad_block = jnp.where(live_four, grad_block, jnp.zeros_like(grad_block))
    shared_dprob = jnp.einsum(
        "slrd,pd->srlp", grad_block, common_values, preferred_element_type=exact
    )
    self_dprob = jnp.einsum(
        "sird,sjd->srij", grad_block, own_response_values, preferred_element_type=exact
    )
    delta_sum = jnp.sum(shared_prob * shared_dprob, axis=-1) + jnp.sum(
        self_prob * self_dprob, axis=-1
    )
    shared_dscore = (shared_prob * (shared_dprob - delta_sum[..., None]) * score_scale).astype(
        jnp.bfloat16
    )
    self_dscore = (self_prob * (self_dprob - delta_sum[..., None]) * score_scale).astype(
        jnp.bfloat16
    )
    query_gradient = jnp.einsum(
        "srlp,pd->slrd", shared_dscore, common_keys, preferred_element_type=exact
    )
    query_gradient = query_gradient + jnp.einsum(
        "srij,sjd->sird", self_dscore, own_response_keys, preferred_element_type=exact
    )
    own_key_gradient = jnp.einsum(
        "srij,sird->sjd", self_dscore, query_block, preferred_element_type=exact
    )
    own_value_gradient = jnp.einsum(
        "srij,sird->sjd", self_weight, grad_block, preferred_element_type=exact
    )
    common_key_gradient = jnp.einsum(
        "srlp,slrd->pd", shared_dscore, query_block, preferred_element_type=exact
    )
    common_value_gradient = jnp.einsum(
        "srlp,slrd->pd", shared_weight, grad_block, preferred_element_type=exact
    )
    return (
        blended_output,
        query_gradient,
        own_key_gradient,
        own_value_gradient,
        common_key_gradient,
        common_value_gradient,
    )


def attend_all(queries, upstream, response_keys, response_values, complete_rows, pre_len, resp_len):
    heads_per_group = QUERY_HEADS // KEY_VALUE_HEADS
    position_count = queries.shape[0] // RESPONSE_LENGTH
    key_width = KEY_VALUE_HEADS * HEAD_WIDTH
    heads_of_queries = queries.reshape(
        position_count, RESPONSE_LENGTH, KEY_VALUE_HEADS, heads_per_group, HEAD_WIDTH
    ).transpose(2, 0, 1, 3, 4)
    gradient_heads = upstream.reshape(
        position_count, RESPONSE_LENGTH, KEY_VALUE_HEADS, heads_per_group, HEAD_WIDTH
    ).transpose(2, 0, 1, 3, 4)
    heads_of_keys = response_keys.reshape(
        position_count, RESPONSE_LENGTH, KEY_VALUE_HEADS, HEAD_WIDTH
    ).transpose(2, 0, 1, 3)
    heads_of_values = response_values.reshape(
        position_count, RESPONSE_LENGTH, KEY_VALUE_HEADS, HEAD_WIDTH
    ).transpose(2, 0, 1, 3)
    common_keys = (
        complete_rows[:, :key_width]
        .reshape(PROMPT_MAXIMUM, KEY_VALUE_HEADS, HEAD_WIDTH)
        .transpose(1, 0, 2)
    )
    common_values = (
        complete_rows[:, key_width:]
        .reshape(PROMPT_MAXIMUM, KEY_VALUE_HEADS, HEAD_WIDTH)
        .transpose(1, 0, 2)
    )

    def per_head(head_items):
        return attend_head(*head_items, pre_len, resp_len)

    results = lax.map(
        per_head,
        (
            heads_of_queries,
            gradient_heads,
            heads_of_keys,
            heads_of_values,
            common_keys,
            common_values,
        ),
    )
    rows_all = position_count * RESPONSE_LENGTH
    blended_output = (
        results[0]
        .transpose(1, 2, 0, 3, 4)
        .reshape(rows_all, QUERY_HEADS * HEAD_WIDTH)
        .astype(jnp.bfloat16)
    )
    query_gradient = (
        results[1]
        .transpose(1, 2, 0, 3, 4)
        .reshape(rows_all, QUERY_HEADS * HEAD_WIDTH)
        .astype(jnp.bfloat16)
    )
    grad_keys = results[2].transpose(1, 2, 0, 3).reshape(rows_all, key_width).astype(jnp.bfloat16)
    grad_values = results[3].transpose(1, 2, 0, 3).reshape(rows_all, key_width).astype(jnp.bfloat16)
    shared_grads = jnp.concatenate(
        [
            results[4].transpose(1, 0, 2).reshape(PROMPT_MAXIMUM, key_width),
            results[5].transpose(1, 0, 2).reshape(PROMPT_MAXIMUM, key_width),
        ],
        axis=1,
    )
    return (blended_output, query_gradient, grad_keys, grad_values, shared_grads)


def swap_gather(shard_rows, device_index):
    for bit_number in range(2):
        partner = swapped(shard_rows, "seq", bit_number)
        is_lower = device_index // (1 << bit_number) % 2 == 0
        shard_rows = jnp.concatenate(
            [jnp.where(is_lower, shard_rows, partner), jnp.where(is_lower, partner, shard_rows)],
            axis=0,
        )
    return shard_rows


def swap_reduce(complete_rows, device_index):
    for bit_number in (1, 0):
        half_rows = complete_rows.shape[0] // 2
        is_lower = device_index // (1 << bit_number) % 2 == 0
        kept_rows = jnp.where(is_lower, complete_rows[:half_rows], complete_rows[half_rows:])
        sent_rows = jnp.where(is_lower, complete_rows[half_rows:], complete_rows[:half_rows])
        complete_rows = kept_rows + swapped(sent_rows, "seq", bit_number)
    return complete_rows


def on_device(
    queries,
    response_keys,
    response_values,
    prompt_key_rows,
    prompt_value_rows,
    upstream,
    prompt_len,
    prompt_owner,
    response_prompt,
    response_len,
):
    device_index = lax.axis_index("seq")
    block_devices = GROUP_RESPONSES // SLOTS
    block_index = device_index // block_devices
    key_width = prompt_key_rows.shape[1]
    prompt_ids = jnp.arange(prompt_owner.shape[0], dtype=jnp.int32)
    is_hosted = prompt_ids == response_prompt[0]
    host_block = jnp.sum(jnp.where(is_hosted, prompt_owner, 0))
    flipped = host_block != block_index
    shard_rows = jnp.concatenate([prompt_key_rows, prompt_value_rows], axis=1)
    pre_length = jnp.sum(jnp.where(is_hosted, prompt_len, 0))
    own_rows = swap_gather(shard_rows, device_index)
    crossed = swapped(own_rows, "seq", 2)
    complete_rows = jnp.where(flipped, crossed, own_rows)
    blended_output, query_gradient, grad_keys, grad_values, shared_grads = attend_all(
        queries, upstream, response_keys, response_values, complete_rows, pre_length, response_len
    )
    crossed_grads = swapped(shared_grads, "seq", 2)
    summed = swap_reduce(jnp.where(flipped, crossed_grads, shared_grads), device_index)
    return (
        blended_output,
        query_gradient,
        grad_keys,
        grad_values,
        summed[:, :key_width],
        summed[:, key_width:],
    )


def solution(mesh):
    placed = (
        P(("groups", "seq"), None),
        P(("groups", "seq"), None),
        P(("groups", "seq"), None),
        P(("groups", "seq"), None),
        P(("groups", "seq"), None),
        P(("groups", "seq"), None),
        P("groups"),
        P("groups"),
        P(("groups", "seq")),
        P(("groups", "seq")),
    )
    return jax.shard_map(
        on_device,
        mesh=mesh,
        in_specs=placed,
        out_specs=(
            P(("groups", "seq"), None),
            P(("groups", "seq"), None),
            P(("groups", "seq"), None),
            P(("groups", "seq"), None),
            P(("groups", "seq"), None),
            P(("groups", "seq"), None),
        ),
        check_vma=False,
    )
```

profile of v0, /device:TPU:0, one launch (start us, length us, event | category | flops | bytes accessed | tf_op | source)
XLA Modules:
  0.0 304.4 jit_solution(5140288796588411397)
XLA Ops:
  0.6 1.0 constant_dynamic-update-slice_fusion.1
  1.6 1.0 constant_dynamic-update-slice_fusion
  3.1 1.5 collective-permute-done
  4.8 3.0 collective-permute-start.1
  7.8 23.6 %collective-permute-done.1 = bf16[512,1024]{1,0:T(8,128)(2,1)} collective-permute-done((bf16[512,1024]{1,0:T(8,128)(2,1)S(1)}, bf16[512,1024]{1,0:T(8,128)(2,1)}, u32[]{:S(2)}, u32[]{:S(2)}) %collective-permute-start.1) | collective-permute-done | bytes 1048608 | tf_op jit(solution)/shard_map/ppermute | solution.py:24
  31.3 1.8 broadcast_select_fusion.3
  33.1 1.5 pad_maximum_fusion
  34.6 1.8 collective-permute-start.2
  36.5 1.5 copy.65
  38.0 2.4 copy.66
  42.6 39.5 %collective-permute-done.2 = bf16[1024,1024]{1,0:T(8,128)(2,1)} collective-permute-done((bf16[1024,1024]{1,0:T(8,128)(2,1)}, bf16[1024,1024]{1,0:T(8,128)(2,1)}, u32[]{:S(2)}, u32[]{:S(2)}) %collective-permute-start.2) | collective-permute-done | bytes 2097184 | tf_op jit(solution)/shard_map/ppermute | solution.py:24
  82.1 2.6 broadcast_select_fusion.1
  86.0 65.0 %while.20 = (s32[]{:T(128)}, bf16[4,2,64,8,128]{4,2,3,1,0:T(8,128)(2,1)}, bf16[4,2,64,8,128]{4,2,3,1,0:T(8,128)(2,1)}, bf16[4,2,64,128]{3,2,1,0:T(8,128)(2,1)S(1...) while((s32[]{:T(128)}, ...), condition=%wide.region_9.10_spmd, body=%wide.region_2.9_spmd.sunk | while | flops 1736648832 | bytes 66648880 | solution.py:145
  86.0 1.0 constant_dynamic-slice_fusion.3
  88.2 0.8 bitcast_reduce_fusion.2
  89.2 1.0 fusion.131
  90.7 1.5 fusion.133
  92.3 1.6 fusion.134
  93.9 0.7 convolution_bitcast_fusion.10
  95.7 1.6 fusion.140
  97.3 1.5 fusion.139
  100.4 1.0 copy-done.2
  101.4 0.9 fusion.138
  102.3 1.0 constant_dynamic-slice_fusion.3
  104.5 0.8 bitcast_reduce_fusion.2
  105.4 1.0 fusion.131
  106.9 1.5 fusion.133
  108.6 1.6 fusion.134
  111.9 1.6 fusion.140
  113.5 1.5 fusion.139
  116.7 1.0 copy-done.2
  117.6 0.9 fusion.138
  118.5 1.0 constant_dynamic-slice_fusion.3
  120.8 0.8 bitcast_reduce_fusion.2
  121.7 1.0 fusion.131
  123.2 1.5 fusion.133
  124.8 1.6 fusion.134
  126.4 0.7 convolution_bitcast_fusion.10
  128.2 1.6 fusion.140
  129.8 1.6 fusion.139
  132.9 1.0 copy-done.2
  133.9 0.9 fusion.138
  134.8 1.0 constant_dynamic-slice_fusion.3
  137.0 0.8 bitcast_reduce_fusion.2
  138.0 1.0 fusion.131
  139.4 1.5 fusion.133
  141.1 1.6 fusion.134
  144.5 1.6 fusion.140
  146.1 1.5 fusion.139
  149.2 1.0 copy-done.2
  150.1 0.9 fusion.138
  151.0 2.0 bitcast_dynamic-update-slice_fusion.1
  153.5 1.6 collective-permute-start.3
  155.1 89.7 %collective-permute-done.3 = f32[1024,1024]{1,0:T(8,128)S(1)} collective-permute-done((f32[1024,1024]{1,0:T(8,128)S(1)}, f32[1024,1024]{1,0:T(8,128)S(1)}, u32[]{:S(2)}, u32[]{:S(2)}) %collective-permute-start.3) | collective-permute-done | bytes 4194336 | tf_op jit(solution)/shard_map/ppermute | solution.py:24
  244.8 1.4 broadcast_select_fusion
  246.6 1.1 collective-permute-start.4
  247.7 44.3 %collective-permute-done.4 = f32[512,1024]{1,0:T(8,128)S(1)} collective-permute-done((f32[512,1024]{1,0:T(8,128)S(1)}, f32[512,1024]{1,0:T(8,128)S(1)}, u32[]{:S(2)}, u32[]{:S(2)}) %collective-permute-start.4) | collective-permute-done | bytes 2097184 | tf_op jit(solution)/shard_map/ppermute | solution.py:24
  292.7 1.1 slice_select_fusion.1
  295.0 1.3 convert_element_type.50
  296.2 1.9 copy.43
  298.2 1.3 convert_element_type.53
  299.4 1.0 copy.45
  301.9 1.5 select_add_fusion.1
  303.4 1.0 fusion.78
  (134 shorter events, 27.3 us)
Async XLA Ops:
  2.6 2.1 collective-permute-start
  4.8 26.5 %collective-permute-start.1 = (bf16[512,1024]{1,0:T(8,128)(2,1)S(1)}, bf16[512,1024]{1,0:T(8,128)(2,1)}, u32[]{:S(2)}, u32[]{:S(2)}) collective-permute-start(bf16[512,1024]{1,0:T(8,128)(2,1)S(1)} %pad_maximum_fusion.1), channel_id=1, source_target_pairs={{0,2},{2,0},{1,3},{3,1},{4,6},{6,4},{5,7},{7,5},{8,10},{10,8},{9,1... | collective-permute-start | bytes 3145736 | tf_op jit(solution)/shard_map/ppermute | solution.py:24
  34.6 47.5 %collective-permute-start.2 = (bf16[1024,1024]{1,0:T(8,128)(2,1)}, bf16[1024,1024]{1,0:T(8,128)(2,1)}, u32[]{:S(2)}, u32[]{:S(2)}) collective-permute-start(bf16[1024,1024]{1,0:T(8,128)(2,1)} %pad_maximum_fusion), channel_id=1, source_target_pairs={{0,4},{4,0},{1,5},{5,1},{2,6},{6,2},{3,7},{7,3},{8,12},{12,8},{9,1... | collective-permute-start | bytes 6291464 | tf_op jit(solution)/shard_map/ppermute | solution.py:24
  36.4 4.0 %copy-start.6 = (bf16[128,512]{1,0:T(8,128)(2,1)S(1)}, bf16[128,512]{1,0:T(8,128)(2,1)}, u32[]{:S(2)}) copy-start(bf16[128,512]{1,0:T(8,128)(2,1)} %param.13) | copy-start | bytes 393220
  36.5 4.1 %copy-start.7 = (bf16[128,512]{1,0:T(8,128)(2,1)S(1)}, bf16[128,512]{1,0:T(8,128)(2,1)}, u32[]{:S(2)}) copy-start(bf16[128,512]{1,0:T(8,128)(2,1)} %param.14) | copy-start | bytes 393220
  38.0 2.6 copy-start.9
  38.0 2.6 copy-start.10
  38.0 3.9 %copy-start.11 = (s32[4]{0:T(128)S(1)}, s32[4]{0:T(128)}, u32[]{:S(2)}) copy-start(s32[4]{0:T(128)} %param.18) | copy-start | bytes 52
  85.1 0.9 copy-start.8
  85.1 0.9 copy-start.12
  93.9 1.2 copy-start.4
  95.4 1.9 copy-start.5
  98.8 1.2 copy-start.1
  100.4 1.0 copy-start.2
  110.1 1.2 copy-start.4
  111.7 1.9 copy-start.5
  115.1 1.2 copy-start.1
  116.6 1.0 copy-start.2
  126.4 1.2 copy-start.4
  128.0 1.8 copy-start.5
  131.4 1.2 copy-start.1
  132.9 1.0 copy-start.2
  142.7 1.2 copy-start.4
  144.2 1.8 copy-start.5
  147.6 1.2 copy-start.1
  149.2 1.0 copy-start.2
  151.0 2.2 copy-start
  153.5 91.3 %collective-permute-start.3 = (f32[1024,1024]{1,0:T(8,128)S(1)}, f32[1024,1024]{1,0:T(8,128)S(1)}, u32[]{:S(2)}, u32[]{:S(2)}) collective-permute-start(f32[1024,1024]{1,0:T(8,128)S(1)} %bitcast_dynamic-update-slice_fusion), channel_id=1, source_target_pairs={{0,4},{4,0},{1,5},{5,1},{2,6},{6,2},{3,7},{7,3},{8,12},{12,8},{9,1... | collective-permute-start | bytes 12582920 | tf_op jit(solution)/shard_map/ppermute | solution.py:24
  246.6 45.4 %collective-permute-start.4 = (f32[512,1024]{1,0:T(8,128)S(1)}, f32[512,1024]{1,0:T(8,128)S(1)}, u32[]{:S(2)}, u32[]{:S(2)}) collective-permute-start(f32[512,1024]{1,0:T(8,128)S(1)} %slice_select_fusion), channel_id=1, source_target_pairs={{0,2},{2,0},{1,3},{3,1},{4,6},{6,4},{5,7},{7,5},{8,10},{10,8},{9,1... | collective-permute-start | bytes 6291464 | tf_op jit(solution)/shard_map/ppermute | solution.py:24
  292.7 1.6 copy-start.3
  293.8 8.1 %collective-permute-start.5 = (f32[256,1024]{1,0:T(8,128)}, f32[256,1024]{1,0:T(8,128)}, u32[]{:S(2)}, u32[]{:S(2)}) collective-permute-start(f32[256,1024]{1,0:T(8,128)} %slice_select_fusion.1), channel_id=1, source_target_pairs={{0,1},{1,0},{2,3},{3,2},{4,5},{5,4},{6,7},{7,6},{8,9},{9,8},{10,11... | collective-permute-start | bytes 3145736 | tf_op jit(solution)/shard_map/ppermute | solution.py:24
where the time goes:
time: 305 us; the launch traced here: 304 us
  waiting for transfers between devices  199 us (65%)
  matrix products  37.8 us (12%)
  local copies, waits for them, and re-layouts  30.8 us (10%)
  other arithmetic  27.1 us (9%)
  starting transfers between devices  7.98 us (3%)
    ppermute x6, waiting for transfers between devices, swapped(): return lax.ppermute(block, axis, route)  199 us
    unnamed x25, local copies, waits for them, and re-layouts  9.86 us
    ppermute x6, starting transfers between devices, swapped(): return lax.ppermute(block, axis, route)  7.98 us
    while x32, local copies, waits for them, and re-layouts  7.9 us
    dot_general x4, matrix products, attend_head(): jnp.einsum('srlp,slrd->pd', shared_weight, grad_block, preferred_element_...  6.36 us
    convert_element_type x4, other arithmetic, attend_head(): (shared_prob * (shared_dprob - delta_sum[..., None]) * score_scale).astyp...  6.25 us
    dot_general x4, matrix products, attend_head(): jnp.einsum('srlp,slrd->pd', shared_dscore, query_block, preferred_element...  6.18 us
  transfers between devices with their start and end apart: 6, of which 5 were waited for; matrix products, arithmetic and copies ran while one was open for 4% of the time, Pallas kernels for 0%

commit v1 on v0

v1 whole, which is shorter than its diff:
```python
import math

import jax
import jax.numpy as jnp
from jax import lax
from jax.experimental import pallas as pl
from jax.experimental.pallas import tpu as pltpu
from jax.sharding import PartitionSpec as P

HEADS = 4
PER_HEAD = 8
WIDTH = 128
RESPONSE = 64
PROMPT = 1024
QUARTER = 256
ROWS = 128
KEYS = PROMPT + ROWS
STACK = 2
CHUNKS = PER_HEAD // STACK
SCALE = 1.0 / math.sqrt(WIDTH)
LOG_SCALE = SCALE * math.log2(math.e)
F32 = jnp.float32
BF16 = jnp.bfloat16
NT = (((1,), (1,)), ((), ()))
NN = (((1,), (0,)), ((), ()))
TN = (((0,), (0,)), ((), ()))


def dot(a, b, dims):
    return lax.dot_general(a, b, dims, preferred_element_type=F32)


def fill_bias(bias, me, pre_len, len0, len1):
    base = me % 4
    row = lax.broadcasted_iota(jnp.int32, (ROWS, QUARTER), 0)
    col = lax.broadcasted_iota(jnp.int32, (ROWS, QUARTER), 1)
    low, high = base % 2, base // 2
    for b, (flip_low, flip_high) in enumerate(((0, 0), (0, 1), (1, 0), (1, 1))):
        lo = 1 - low if flip_low else low
        hi = 1 - high if flip_high else high
        position = (hi * 2 + lo) * QUARTER + col
        bias[:, b * QUARTER : (b + 1) * QUARTER] = jnp.where(position < pre_len, 0.0, -1e30)
    row = lax.broadcasted_iota(jnp.int32, (ROWS, ROWS), 0)
    col = lax.broadcasted_iota(jnp.int32, (ROWS, ROWS), 1)
    first = (row < RESPONSE) & (col <= row) & (col < len0)
    second = (col >= RESPONSE) & (col <= row) & (col - RESPONSE < len1)
    bias[:, PROMPT:] = jnp.where(first | second, 0.0, -1e30)


def attend_chunk(g, chunk, q_ref, up_ref, kv, bias, live, out_ref, gq_ref, acc):
    column = g * PER_HEAD * WIDTH + chunk * STACK * WIDTH
    start = column if isinstance(column, int) else pl.multiple_of(column, STACK * WIDTH)
    q_wide = q_ref[:, pl.ds(start, STACK * WIDTH)]
    up_wide = up_ref[:, pl.ds(start, STACK * WIDTH)]
    q = jnp.concatenate([q_wide[:, i * WIDTH : (i + 1) * WIDTH] for i in range(STACK)], axis=0)
    up = jnp.concatenate([up_wide[:, i * WIDTH : (i + 1) * WIDTH] for i in range(STACK)], axis=0)
    live_rows = jnp.concatenate([live] * STACK, axis=0) > 0.5
    up = jnp.where(live_rows, up.astype(F32), 0.0).astype(BF16)
    keys = kv[g, 0]
    values = kv[g, 1]
    s = dot(q, keys, NT).reshape(STACK, ROWS, KEYS) + bias[...][None]
    s = s.reshape(STACK * ROWS, KEYS)
    top = jnp.max(s, axis=1, keepdims=True)
    e = jnp.exp2((s - top) * LOG_SCALE)
    inverse = 1.0 / jnp.sum(e, axis=1, keepdims=True)
    p = e * inverse
    weight = p.astype(BF16)
    dp = dot(up, values, NT)
    delta = jnp.sum(p * dp, axis=1, keepdims=True)
    ds = (p * (dp - delta)).astype(BF16)
    o = jnp.where(live_rows, dot(weight, values, NN), 0.0).astype(BF16)
    dq = (dot(ds, keys, NN) * SCALE).astype(BF16)
    for i in range(STACK):
        place = pl.ds(start + i * WIDTH, WIDTH)
        out_ref[:, place] = o[i * ROWS : (i + 1) * ROWS]
        gq_ref[:, place] = dq[i * ROWS : (i + 1) * ROWS]
    dk = dot(q, ds, TN)
    dv = dot(up, weight, TN)
    acc[g, 0] += dk
    acc[g, 1] += dv


def kernel(
    plen_ref, owner_ref, rprompt_ref, rlen_ref,
    q_ref, up_ref, rk_ref, rv_ref, pk_ref, pv_ref,
    out_ref, gq_ref, grk_ref, grv_ref, gpk_ref, gpv_ref,
    kv, own, zbuf, bias, live, acc, crecv, ysend, yrecv, final, zsend, zrecv,
    za, ya, ca, fa, cb, yb, zb,
):
    me = lax.axis_index("seq")
    core = me + 1 - 2 * (me % 2)
    ypart = me + 2 - 4 * (me // 2 % 2)
    zpart = me + 4 - 8 * (me // 4 % 2)

    barrier = pltpu.get_barrier_semaphore()
    for other in (core, ypart, zpart):
        pl.semaphore_signal(barrier, inc=1, device_id={"seq": other})

    for g in range(HEADS):
        columns = slice(g * WIDTH, (g + 1) * WIDTH)
        own[g, 0] = pk_ref[:, columns]
        own[g, 1] = pv_ref[:, columns]
    pl.semaphore_wait(barrier, 3)

    def send(src, dst, sems, index, other):
        copy = pltpu.make_async_remote_copy(
            src_ref=src, dst_ref=dst, send_sem=sems.at[0, index], recv_sem=sems.at[1, index],
            device_id={"seq": other},
        )
        copy.start()
        return copy

    z_in = [send(own.at[g], zbuf.at[g], za, g, zpart) for g in range(HEADS)]

    prompt = rprompt_ref[0]
    pre_len = plen_ref[prompt]
    flipped = owner_ref[prompt] != me // 4
    len0, len1 = rlen_ref[0], rlen_ref[1]
    for g in range(HEADS):
        columns = slice(g * WIDTH, (g + 1) * WIDTH)
        kv[g, 0, PROMPT:] = rk_ref[:, columns]
        kv[g, 1, PROMPT:] = rv_ref[:, columns]
    fill_bias(bias, me, pre_len, len0, len1)
    row = lax.broadcasted_iota(jnp.int32, (ROWS, WIDTH), 0)
    live[...] = jnp.where(((row < RESPONSE) & (row < len0)) | ((row >= RESPONSE) & (row - RESPONSE < len1)), 1.0, 0.0)
    acc[...] = jnp.zeros_like(acc)

    y_in, c_in, f_in = [], [], []
    c_out, y_out, z_out = [], [], []

    def gather_first(g):
        z_in[g].wait_recv()
        kv[g, :, 0:QUARTER] = jnp.where(flipped, zbuf[g], own[g])
        y_in.append(send(kv.at[g, :, 0:QUARTER], kv.at[g, :, QUARTER : 2 * QUARTER], ya, g, ypart))
        c_in.append(send(kv.at[g, :, 0:QUARTER], kv.at[g, :, 2 * QUARTER : 3 * QUARTER], ca, g, core))

    def gather_second(g):
        y_in[g].wait_recv()
        f_in.append(send(kv.at[g, :, QUARTER : 2 * QUARTER], kv.at[g, :, 3 * QUARTER : PROMPT], fa, g, core))

    def gather_last(g):
        c_in[g].wait_recv()
        f_in[g].wait_recv()

    def attend(g, low, high):
        def body(chunk, carry):
            attend_chunk(g, chunk, q_ref, up_ref, kv, bias, live[...], out_ref, gq_ref, acc)
            return carry

        lax.fori_loop(low, high, body, 0)

    def reduce_core(g):
        c_out.append(send(acc.at[g, :, :, 2 * QUARTER : PROMPT], crecv.at[g], cb, g, core))
        columns = slice(g * WIDTH, (g + 1) * WIDTH)
        grk_ref[:, columns] = (acc[g, 0, :, PROMPT:].T * SCALE).astype(BF16)
        grv_ref[:, columns] = acc[g, 1, :, PROMPT:].T.astype(BF16)

    def reduce_y(g):
        c_out[g].wait_recv()
        ysend[g] = (acc[g, :, :, QUARTER : 2 * QUARTER] + crecv[g, :, :, QUARTER:]).astype(BF16)
        y_out.append(send(ysend.at[g], yrecv.at[g], yb, g, ypart))

    def reduce_z(g):
        y_out[g].wait_recv()
        total = acc[g, :, :, 0:QUARTER] + crecv[g, :, :, 0:QUARTER] + yrecv[g].astype(F32)
        final[g] = total
        zsend[g] = total.astype(BF16)
        z_out.append(send(zsend.at[g], zrecv.at[g], zb, g, zpart))

    def finish(g):
        z_out[g].wait_recv()
        total = jnp.where(flipped, zrecv[g].astype(F32), final[g])
        columns = slice(g * WIDTH, (g + 1) * WIDTH)
        gpk_ref[:, columns] = total[0].T * SCALE
        gpv_ref[:, columns] = total[1].T

    half = CHUNKS // 2
    gather_first(0)
    gather_second(0)
    gather_first(1)
    gather_last(0)
    for g in range(HEADS):
        attend(g, 0, half)
        if g + 1 < HEADS:
            gather_second(g + 1)
        if g + 2 < HEADS:
            gather_first(g + 2)
        if g >= 1:
            reduce_y(g - 1)
        if g >= 2:
            finish(g - 2)
        attend(g, half, CHUNKS)
        if g + 1 < HEADS:
            gather_last(g + 1)
        reduce_core(g)
        if g >= 1:
            reduce_z(g - 1)
    last = HEADS - 1
    reduce_y(last)
    reduce_z(last)
    finish(last - 1)
    finish(last)
    for copy in z_in + y_in + c_in + f_in + c_out + y_out + z_out:
        copy.wait_send()


def on_device(queries, response_keys, response_values, prompt_key_rows, prompt_value_rows, upstream,
              prompt_len, prompt_owner, response_prompt, response_len):
    smem = pl.BlockSpec(memory_space=pltpu.SMEM)
    vmem = pl.BlockSpec(memory_space=pltpu.VMEM)
    shape = jax.ShapeDtypeStruct
    wide = shape(queries.shape, BF16)
    thin = shape(response_keys.shape, BF16)
    prefix = shape(prompt_key_rows.shape, F32)
    pair = pltpu.SemaphoreType.DMA((2, HEADS))
    return tuple(pl.pallas_call(
        kernel,
        out_shape=(wide, wide, thin, thin, prefix, prefix),
        in_specs=[smem] * 4 + [vmem] * 6,
        out_specs=[vmem] * 6,
        scratch_shapes=[
            pltpu.VMEM((HEADS, 2, KEYS, WIDTH), BF16),
            pltpu.VMEM((HEADS, 2, QUARTER, WIDTH), BF16),
            pltpu.VMEM((HEADS, 2, QUARTER, WIDTH), BF16),
            pltpu.VMEM((ROWS, KEYS), F32),
            pltpu.VMEM((ROWS, WIDTH), F32),
            pltpu.VMEM((HEADS, 2, WIDTH, KEYS), F32),
            pltpu.VMEM((HEADS, 2, WIDTH, 2 * QUARTER), F32),
            pltpu.VMEM((HEADS, 2, WIDTH, QUARTER), BF16),
            pltpu.VMEM((HEADS, 2, WIDTH, QUARTER), BF16),
            pltpu.VMEM((HEADS, 2, WIDTH, QUARTER), F32),
            pltpu.VMEM((HEADS, 2, WIDTH, QUARTER), BF16),
            pltpu.VMEM((HEADS, 2, WIDTH, QUARTER), BF16),
        ] + [pair] * 7,
        compiler_params=pltpu.CompilerParams(
            collective_id=0, has_side_effects=True, vmem_limit_bytes=56 * 1024 * 1024
        ),
        cost_estimate=pl.CostEstimate(flops=7 * 10**9, bytes_accessed=7 * 10**6, transcendentals=5 * 10**6),
        name="grouped",
    )(prompt_len, prompt_owner, response_prompt, response_len,
      queries, upstream, response_keys, response_values, prompt_key_rows, prompt_value_rows))


def solution(mesh):
    rows = P(("groups", "seq"), None)
    return jax.shard_map(
        on_device,
        mesh=mesh,
        in_specs=(rows,) * 6 + (P("groups"), P("groups"), P(("groups", "seq")), P(("groups", "seq"))),
        out_specs=(rows,) * 6,
        check_vma=False,
    )
```

time: 305 us -> 68.6 us (0.22)
  waiting for transfers between devices: 199 us -> 0 us
  Pallas kernels: 0 us -> 60.7 us
  matrix products: 37.8 us -> 0 us
  other arithmetic: 27.1 us -> 0 us
  local copies, waits for them, and re-layouts: 30.8 us -> 7.01 us
  starting transfers between devices: 7.98 us -> 0 us
    ppermute x6 -> x0, waiting for transfers between devices: 199 us -> none  [swapped(): return lax.ppermute(block, axis, route)]
    pallas_call x0 -> x1, Pallas kernels: none -> 60.7 us  [on_device(): pl.pallas_call(kernel, out_shape=(wide, wide, thin, thin, prefix, prefix)...]
    dot_general x48 -> x0, matrix products: 37.8 us -> none  [the longest x4 6.36 us: attend_head(): jnp.einsum('srlp,slrd->pd', shared_weight, grad_block, preferred_element_...]
    ppermute x6 -> x0, starting transfers between devices: 7.98 us -> none  [swapped(): return lax.ppermute(block, axis, route)]
    while x34 -> x0, local copies, waits for them, and re-layouts: 7.94 us -> none
    select_n x6 -> x0, other arithmetic: 7.33 us -> none  [the longest x1 2.58 us: on_device(): complete_rows = jnp.where(flipped, crossed, own_rows)]
    convert_element_type x8 -> x0, other arithmetic: 7 us -> none  [the longest x4 6.25 us: attend_head(): (shared_prob * (shared_dprob - delta_sum[..., None]) * score_scale).astyp...]
    convert_element_type x6 -> x0, local copies, waits for them, and re-layouts: 6.24 us -> none  [the longest x2 3.18 us: attend_all(): query_gradient = results[1].transpose(1, 2, 0, 3, 4).reshape(rows_all, QU...]
  transfers between devices with their start and end apart: 6 -> 0, of which waited for: 5 -> 0; matrix products, arithmetic and copies ran while one was open for 4% -> 0% of each run, Pallas kernels for 0% -> 0%
where the time goes in v1:
time: 68.6 us; the launch traced here: 68.4 us
  Pallas kernels  60.7 us (88%)
  local copies, waits for them, and re-layouts  7.01 us (10%)
    pallas_call x1, Pallas kernels, on_device(): pl.pallas_call(kernel, out_shape=(wide, wide, thin, thin, prefix, prefix)...  60.7 us
    unnamed x16, local copies, waits for them, and re-layouts  7.01 us

profile of v1, /device:TPU:0, one launch (start us, length us, event | category | flops | bytes accessed | tf_op | source)
XLA Modules:
  0.0 68.4 jit_solution(17385723032210439351)
XLA Ops:
  0.6 60.7 %grouped.1 = (bf16[128,4096]{1,0:T(8,128)(2,1)}, bf16[128,4096]{1,0:T(8,128)(2,1)}, bf16[128,512]{1,0:T(8,128)(2,1)}, bf16[128,512]{1,0:T(8,128)(2,1)}, f32[256,512]{1,0:T(8,128)}, /*index=5*/f32[256,512]{1,0:T(8,128)}) custom-call(s32[4]{0:T(128)} %plen_ref.1, s32[4]{0:T(128)} %owner_ref.1, s32[2]{0:T(128)} %rprompt_ref.1, s32[2]{0:T(128)} %rlen_ref.1, ...), custom_call_target="tpu_custom_call" | custom-call | flops 7000000000 | bytes 7000000 | tf_op jit(solution)/shard_map/grouped/pallas_call | solution.py:216
  61.3 0.0 copy-start
  61.3 2.4 %copy.22 = bf16[128,4096]{1,0:T(8,128)(2,1)} copy(bf16[128,4096]{1,0:T(8,128)(2,1)} %get-tuple-element.12) | data formatting | bytes 2097152
  63.7 0.0 copy-done
  63.7 0.0 copy-start.4
  63.7 0.0 copy-start.2
  63.7 1.0 %copy.23 = bf16[128,4096]{1,0:T(8,128)(2,1)} copy(bf16[128,4096]{1,0:T(8,128)(2,1)S(1)} %copy-done) | data formatting | bytes 2097152
  64.7 0.0 copy-done.4
  64.7 0.0 copy-start.3
  64.7 0.7 copy.24
  65.4 0.3 copy-done.3
  65.7 0.7 copy.25
  66.3 0.0 copy-done.2
  66.3 0.0 copy-start.1
  66.3 0.8 %copy.26 = f32[256,512]{1,0:T(8,128)} copy(f32[256,512]{1,0:T(8,128)S(1)} %copy-done.2) | data formatting | bytes 1048576
  67.1 0.4 copy-done.1
  67.6 0.8 %copy.27 = f32[256,512]{1,0:T(8,128)} copy(f32[256,512]{1,0:T(8,128)S(1)} %copy-done.1) | data formatting | bytes 1048576
Async XLA Ops:
  61.3 2.4 %copy-start = (bf16[128,4096]{1,0:T(8,128)(2,1)S(1)}, bf16[128,4096]{1,0:T(8,128)(2,1)}, u32[]{:S(2)}) copy-start(bf16[128,4096]{1,0:T(8,128)(2,1)} %get-tuple-element.13) | copy-start | bytes 3145732
  63.7 1.0 %copy-start.4 = (bf16[128,512]{1,0:T(8,128)(2,1)S(1)}, bf16[128,512]{1,0:T(8,128)(2,1)}, u32[]{:S(2)}) copy-start(bf16[128,512]{1,0:T(8,128)(2,1)} %get-tuple-element.14) | copy-start | bytes 393220
  63.7 2.6 %copy-start.2 = (f32[256,512]{1,0:T(8,128)S(1)}, f32[256,512]{1,0:T(8,128)}, u32[]{:S(2)}) copy-start(f32[256,512]{1,0:T(8,128)} %get-tuple-element.16) | copy-start | bytes 1572868
  64.7 1.0 %copy-start.3 = (bf16[128,512]{1,0:T(8,128)(2,1)S(1)}, bf16[128,512]{1,0:T(8,128)(2,1)}, u32[]{:S(2)}) copy-start(bf16[128,512]{1,0:T(8,128)(2,1)} %get-tuple-element.15) | copy-start | bytes 393220
  66.3 1.2 %copy-start.1 = (f32[256,512]{1,0:T(8,128)S(1)}, f32[256,512]{1,0:T(8,128)}, u32[]{:S(2)}) copy-start(f32[256,512]{1,0:T(8,128)} %get-tuple-element.17) | copy-start | bytes 1572868

commit v2 on v1

v2 whole, which is shorter than its diff:
```python
import functools
import math

import jax
import jax.numpy as jnp
from jax import lax
from jax.experimental import pallas as pl
from jax.experimental.pallas import tpu as pltpu
from jax.sharding import PartitionSpec as P

HEADS = 4
PER_HEAD = 8
WIDTH = 128
RESPONSE = 64
PROMPT = 1024
QUARTER = 256
ROWS = 128
KEYS = PROMPT + ROWS
STACK = 4
CHUNKS = PER_HEAD // STACK
SCALE = 1.0 / math.sqrt(WIDTH)
LOG_SCALE = SCALE * math.log2(math.e)
F32 = jnp.float32
BF16 = jnp.bfloat16
NT = (((1,), (1,)), ((), ()))
NN = (((1,), (0,)), ((), ()))
TN = (((0,), (0,)), ((), ()))


def dot(a, b, dims):
    return lax.dot_general(a, b, dims, preferred_element_type=F32)


def fill_bias(bias, me, pre_len, len0, len1):
    base = me % 4
    row = lax.broadcasted_iota(jnp.int32, (ROWS, QUARTER), 0)
    col = lax.broadcasted_iota(jnp.int32, (ROWS, QUARTER), 1)
    low, high = base % 2, base // 2
    for b, (flip_low, flip_high) in enumerate(((0, 0), (0, 1), (1, 0), (1, 1))):
        lo = 1 - low if flip_low else low
        hi = 1 - high if flip_high else high
        position = (hi * 2 + lo) * QUARTER + col
        bias[:, b * QUARTER : (b + 1) * QUARTER] = jnp.where(position < pre_len, 0.0, -1e30)
    row = lax.broadcasted_iota(jnp.int32, (ROWS, ROWS), 0)
    col = lax.broadcasted_iota(jnp.int32, (ROWS, ROWS), 1)
    first = (row < RESPONSE) & (col <= row) & (col < len0)
    second = (col >= RESPONSE) & (col <= row) & (col - RESPONSE < len1)
    bias[:, PROMPT:] = jnp.where(first | second, 0.0, -1e30)


def attend_chunk(g, chunk, q_ref, up_ref, kv, bias, live, out_ref, gq_ref, acc, before_values, after_values):
    start = g * PER_HEAD * WIDTH + chunk * STACK * WIDTH
    heads = [slice(start + i * WIDTH, start + (i + 1) * WIDTH) for i in range(STACK)]
    q = jnp.concatenate([q_ref[:, h] for h in heads], axis=0)
    up = jnp.concatenate([up_ref[:, h] for h in heads], axis=0)
    live_rows = jnp.concatenate([live] * STACK, axis=0) > 0.5
    up = jnp.where(live_rows, up.astype(F32), 0.0).astype(BF16)
    keys = kv[g, 0]
    s = dot(q, keys, NT).reshape(STACK, ROWS, KEYS) + bias[...][None]
    s = s.reshape(STACK * ROWS, KEYS)
    top = jnp.max(s, axis=1, keepdims=True)
    e = jnp.exp2((s - top) * LOG_SCALE)
    inverse = 1.0 / jnp.sum(e, axis=1, keepdims=True)
    p = e * inverse
    weight = p.astype(BF16)
    before_values()
    dv = dot(up, weight, TN)
    if chunk == 0:
        acc[g, 1] = dv
    else:
        acc[g, 1] += dv
    after_values()
    values = kv[g, 1]
    dp = dot(up, values, NT)
    delta = jnp.sum(p * dp, axis=1, keepdims=True)
    ds = (p * (dp - delta)).astype(BF16)
    dk = dot(q, ds, TN)
    if chunk == 0:
        acc[g, 0] = dk
    else:
        acc[g, 0] += dk
    o = jnp.where(live_rows, dot(weight, values, NN), 0.0).astype(BF16)
    dq = (dot(ds, keys, NN) * SCALE).astype(BF16)
    for i, h in enumerate(heads):
        out_ref[:, h] = o[i * ROWS : (i + 1) * ROWS]
        gq_ref[:, h] = dq[i * ROWS : (i + 1) * ROWS]


def kernel(
    plen_ref, owner_ref, rprompt_ref, rlen_ref,
    q_hbm, up_hbm, rk_ref, rv_ref, pk_ref, pv_ref,
    out_ref, gq_ref, grk_ref, grv_ref, gpk_ref, gpv_ref,
    q_ref, up_ref, kv, zbuf, bias, live, acc, crecv, ysend, yrecv, final, zsend, zrecv,
    za, ya, ca, fa, cb, yb, zb, local,
):
    me = lax.axis_index("seq")
    core = me + 1 - 2 * (me % 2)
    ypart = me + 2 - 4 * (me // 2 % 2)
    zpart = me + 4 - 8 * (me // 4 % 2)
    prompt_refs = (pk_ref, pv_ref)
    response_refs = (rk_ref, rv_ref)

    barrier = pltpu.get_barrier_semaphore()
    for other in (zpart, ypart, core):
        pl.semaphore_signal(barrier, inc=1, device_id={"seq": other})
    loads = [
        pltpu.make_async_copy(q_hbm, q_ref, local.at[0]),
        pltpu.make_async_copy(up_hbm, up_ref, local.at[1]),
    ]
    for load in loads:
        load.start()
    pl.semaphore_wait(barrier, 3)

    def columns(g):
        return slice(g * WIDTH, (g + 1) * WIDTH)

    def send(src, dst, sems, g, k, other):
        copy = pltpu.make_async_remote_copy(
            src_ref=src, dst_ref=dst, send_sem=sems.at[0, 2 * g + k], recv_sem=sems.at[1, 2 * g + k],
            device_id={"seq": other},
        )
        copy.start()
        return copy

    z_in, y_in, c_in, f_in, c_out, y_out, z_out = ({} for _ in range(7))
    for g in range(HEADS):
        for k in range(2):
            z_in[g, k] = send(prompt_refs[k].at[:, columns(g)], zbuf.at[g, k], za, g, k, zpart)

    prompt = rprompt_ref[0]
    pre_len = plen_ref[prompt]
    flipped = owner_ref[prompt] != me // 4
    len0, len1 = rlen_ref[0], rlen_ref[1]
    for g in range(HEADS):
        for k in range(2):
            kv[g, k, PROMPT:] = response_refs[k][:, columns(g)]
    fill_bias(bias, me, pre_len, len0, len1)
    row = lax.broadcasted_iota(jnp.int32, (ROWS, WIDTH), 0)
    live[...] = jnp.where(((row < RESPONSE) & (row < len0)) | ((row >= RESPONSE) & (row - RESPONSE < len1)), 1.0, 0.0)

    def gather_first(g, k):
        z_in[g, k].wait_recv()
        kv[g, k, 0:QUARTER] = jnp.where(flipped, zbuf[g, k], prompt_refs[k][:, columns(g)])
        mine = kv.at[g, k, 0:QUARTER]
        y_in[g, k] = send(mine, kv.at[g, k, QUARTER : 2 * QUARTER], ya, g, k, ypart)
        c_in[g, k] = send(mine, kv.at[g, k, 2 * QUARTER : 3 * QUARTER], ca, g, k, core)

    def gather_second(g, k):
        y_in[g, k].wait_recv()
        f_in[g, k] = send(kv.at[g, k, QUARTER : 2 * QUARTER], kv.at[g, k, 3 * QUARTER : PROMPT], fa, g, k, core)

    def gather_last(g, k):
        c_in[g, k].wait_recv()
        f_in[g, k].wait_recv()

    def reduce_core(g, k):
        c_out[g, k] = send(acc.at[g, k, :, 2 * QUARTER : PROMPT], crecv.at[g, k], cb, g, k, core)

    def own_grads(g):
        grk_ref[:, columns(g)] = (acc[g, 0, :, PROMPT:].T * SCALE).astype(BF16)
        grv_ref[:, columns(g)] = acc[g, 1, :, PROMPT:].T.astype(BF16)

    def reduce_y(g, k):
        c_out[g, k].wait_recv()
        ysend[g, k] = (acc[g, k, :, QUARTER : 2 * QUARTER] + crecv[g, k, :, QUARTER:]).astype(BF16)
        y_out[g, k] = send(ysend.at[g, k], yrecv.at[g, k], yb, g, k, ypart)

    def reduce_z(g, k):
        y_out[g, k].wait_recv()
        total = acc[g, k, :, 0:QUARTER] + crecv[g, k, :, 0:QUARTER] + yrecv[g, k].astype(F32)
        final[g, k] = total
        zsend[g, k] = total.astype(BF16)
        z_out[g, k] = send(zsend.at[g, k], zrecv.at[g, k], zb, g, k, zpart)

    def finish(g, k):
        z_out[g, k].wait_recv()
        total = jnp.where(flipped, zrecv[g, k].astype(F32), final[g, k])
        if k == 0:
            gpk_ref[:, columns(g)] = total.T * SCALE
        else:
            gpv_ref[:, columns(g)] = total.T

    def both(step, g):
        for k in (1, 0):
            step(g, k)

    def nothing():
        pass

    def attend(g, chunk, before=nothing, after=nothing):
        attend_chunk(g, chunk, q_ref, up_ref, kv, bias, live[...], out_ref, gq_ref, acc, before, after)

    last = HEADS - 1
    gather_first(0, 0)
    gather_first(0, 1)
    gather_second(0, 0)
    gather_first(1, 0)
    gather_second(0, 1)
    gather_first(1, 1)
    for load in loads:
        load.wait()
    gather_last(0, 0)
    for g in range(HEADS):
        attend(g, 0, before=functools.partial(gather_last, g, 1) if g == 0 else nothing)
        if g == 0:
            both(gather_second, 1)
            both(gather_first, 2)
        elif g + 1 < HEADS:
            both(gather_second, g + 1)
        if g >= 1:
            both(reduce_y, g - 1)
        if g >= 2:
            both(reduce_z, g - 2)
        if g >= 3:
            both(finish, g - 3)
        attend(g, 1, after=functools.partial(reduce_core, g, 1))
        reduce_core(g, 0)
        if g == last:
            reduce_y(g, 1)
            reduce_y(g, 0)
        own_grads(g)
        if g + 1 < HEADS:
            both(gather_last, g + 1)
        if g + 3 < HEADS:
            both(gather_first, g + 3)
    both(reduce_z, last - 1)
    both(finish, last - 2)
    both(reduce_z, last)
    both(finish, last - 1)
    both(finish, last)
    for group in (z_in, y_in, c_in, f_in, c_out, y_out, z_out):
        for copy in group.values():
            copy.wait_send()


def on_device(queries, response_keys, response_values, prompt_key_rows, prompt_value_rows, upstream,
              prompt_len, prompt_owner, response_prompt, response_len):
    smem = pl.BlockSpec(memory_space=pltpu.SMEM)
    vmem = pl.BlockSpec(memory_space=pltpu.VMEM)
    shape = jax.ShapeDtypeStruct
    wide = shape(queries.shape, BF16)
    thin = shape(response_keys.shape, BF16)
    prefix = shape(prompt_key_rows.shape, F32)
    pair = pltpu.SemaphoreType.DMA((2, 2 * HEADS))
    return tuple(pl.pallas_call(
        kernel,
        out_shape=tuple(pltpu.VMEM(o.shape, o.dtype) for o in (wide, wide, thin, thin, prefix, prefix)),
        in_specs=[smem] * 4 + [pl.BlockSpec(memory_space=pl.ANY)] * 2 + [vmem] * 4,
        out_specs=[vmem] * 6,
        scratch_shapes=[
            pltpu.VMEM(queries.shape, BF16),
            pltpu.VMEM(queries.shape, BF16),
            pltpu.VMEM((HEADS, 2, KEYS, WIDTH), BF16),
            pltpu.VMEM((HEADS, 2, QUARTER, WIDTH), BF16),
            pltpu.VMEM((ROWS, KEYS), F32),
            pltpu.VMEM((ROWS, WIDTH), F32),
            pltpu.VMEM((HEADS, 2, WIDTH, KEYS), F32),
            pltpu.VMEM((HEADS, 2, WIDTH, 2 * QUARTER), F32),
            pltpu.VMEM((HEADS, 2, WIDTH, QUARTER), BF16),
            pltpu.VMEM((HEADS, 2, WIDTH, QUARTER), BF16),
            pltpu.VMEM((HEADS, 2, WIDTH, QUARTER), F32),
            pltpu.VMEM((HEADS, 2, WIDTH, QUARTER), BF16),
            pltpu.VMEM((HEADS, 2, WIDTH, QUARTER), BF16),
        ] + [pair] * 7 + [pltpu.SemaphoreType.DMA((2,))],
        compiler_params=pltpu.CompilerParams(
            collective_id=0, has_side_effects=True, vmem_limit_bytes=56 * 1024 * 1024
        ),
        cost_estimate=pl.CostEstimate(flops=7 * 10**9, bytes_accessed=7 * 10**6, transcendentals=5 * 10**6),
        name="grouped",
    )(prompt_len, prompt_owner, response_prompt, response_len,
      queries, upstream, response_keys, response_values, prompt_key_rows, prompt_value_rows))


def solution(mesh):
    rows = P(("groups", "seq"), None)
    return jax.shard_map(
        on_device,
        mesh=mesh,
        in_specs=(rows,) * 6 + (P("groups"), P("groups"), P(("groups", "seq")), P(("groups", "seq"))),
        out_specs=(rows,) * 6,
        check_vma=False,
    )
```

time: 68.6 us -> 54.5 us (0.79)
  Pallas kernels: 60.7 us -> 48.8 us
  local copies, waits for them, and re-layouts: 7.01 us -> 4.84 us
    pallas_call x1, Pallas kernels: 60.7 us -> 48.8 us  [on_device(): pl.pallas_call(kernel, out_shape=tuple((pltpu.VMEM(o.shape, o.dtype) for...]
    unnamed x16 -> x6, local copies, waits for them, and re-layouts: 7.01 us -> 4.84 us
where the time goes in v2:
time: 54.5 us; the launch traced here: 54.3 us
  Pallas kernels  48.8 us (90%)
  local copies, waits for them, and re-layouts  4.84 us (9%)
  between operations  0.65 us (1%)
    pallas_call x1, Pallas kernels, on_device(): pl.pallas_call(kernel, out_shape=tuple((pltpu.VMEM(o.shape, o.dtype) for...  48.8 us
    unnamed x6, local copies, waits for them, and re-layouts  4.84 us

profile of v2, /device:TPU:0, one launch (start us, length us, event | category | flops | bytes accessed | tf_op | source)
XLA Modules:
  0.0 54.3 jit_solution(16744547864372093926)
XLA Ops:
  0.6 48.8 %grouped.1 = (bf16[128,4096]{1,0:T(8,128)(2,1)S(1)}, bf16[128,4096]{1,0:T(8,128)(2,1)S(1)}, bf16[128,512]{1,0:T(8,128)(2,1)S(1)}, bf16[128,512]{1,0:T(8,128)(2,1...) custom-call(s32[4]{0:T(128)} %plen_ref.1, s32[4]{0:T(128)} %owner_ref.1, s32[2]{0:T(128)} %rprompt_ref.1, ...), custom_call_target="tpu_custom_call" | custom-call | flops 7000000000 | bytes 7000000 | tf_op jit(solution)/shard_map/grouped/pallas_call | solution.py:245
  49.5 1.0 %copy.22 = bf16[128,4096]{1,0:T(8,128)(2,1)} copy(bf16[128,4096]{1,0:T(8,128)(2,1)S(1)} %get-tuple-element.6) | data formatting | bytes 2097152
  50.4 0.7 %copy.24 = bf16[128,512]{1,0:T(8,128)(2,1)} copy(bf16[128,512]{1,0:T(8,128)(2,1)S(1)} %get-tuple-element.8) | data formatting | bytes 262144
  51.1 0.7 %copy.25 = bf16[128,512]{1,0:T(8,128)(2,1)} copy(bf16[128,512]{1,0:T(8,128)(2,1)S(1)} %get-tuple-element.9) | data formatting | bytes 262144
  51.7 0.8 %copy.26 = f32[256,512]{1,0:T(8,128)} copy(f32[256,512]{1,0:T(8,128)S(1)} %get-tuple-element.10) | data formatting | bytes 1048576
  52.5 0.8 %copy.27 = f32[256,512]{1,0:T(8,128)} copy(f32[256,512]{1,0:T(8,128)S(1)} %get-tuple-element.11) | data formatting | bytes 1048576
  53.3 1.0 %copy.23 = bf16[128,4096]{1,0:T(8,128)(2,1)} copy(bf16[128,4096]{1,0:T(8,128)(2,1)S(1)} %get-tuple-element.7) | data formatting | bytes 2097152

commit v3 on v2

--- a/solution.py
+++ b/solution.py
@@ -48,7 +48,7 @@
     bias[:, PROMPT:] = jnp.where(first | second, 0.0, -1e30)
 
 
-def attend_chunk(g, chunk, q_ref, up_ref, kv, bias, live, out_ref, gq_ref, acc, before_values, after_values):
+def attend_chunk(g, chunk, q_ref, up_ref, kv, bias, live, out_ref, gq_ref, acc, before_values, after_values, after_keys):
     start = g * PER_HEAD * WIDTH + chunk * STACK * WIDTH
     heads = [slice(start + i * WIDTH, start + (i + 1) * WIDTH) for i in range(STACK)]
     q = jnp.concatenate([q_ref[:, h] for h in heads], axis=0)
@@ -79,6 +79,7 @@
         acc[g, 0] = dk
     else:
         acc[g, 0] += dk
+    after_keys()
     o = jnp.where(live_rows, dot(weight, values, NN), 0.0).astype(BF16)
     dq = (dot(ds, keys, NN) * SCALE).astype(BF16)
     for i, h in enumerate(heads):
@@ -187,10 +188,16 @@
     def nothing():
         pass
 
-    def attend(g, chunk, before=nothing, after=nothing):
-        attend_chunk(g, chunk, q_ref, up_ref, kv, bias, live[...], out_ref, gq_ref, acc, before, after)
+    def attend(g, chunk, before=nothing, after=nothing, keyed=nothing):
+        attend_chunk(g, chunk, q_ref, up_ref, kv, bias, live[...], out_ref, gq_ref, acc, before, after, keyed)
 
     last = HEADS - 1
+
+    def after_key(g):
+        reduce_core(g, 0)
+        if g == last:
+            reduce_y(g, 1)
+
     gather_first(0, 0)
     gather_first(0, 1)
     gather_second(0, 0)
@@ -213,10 +220,8 @@
             both(reduce_z, g - 2)
         if g >= 3:
             both(finish, g - 3)
-        attend(g, 1, after=functools.partial(reduce_core, g, 1))
-        reduce_core(g, 0)
+        attend(g, 1, nothing, functools.partial(reduce_core, g, 1), functools.partial(after_key, g))
         if g == last:
-            reduce_y(g, 1)
             reduce_y(g, 0)
         own_grads(g)
         if g + 1 < HEADS:

time: 54.5 us -> 53.9 us (0.989)
  Pallas kernels: 48.8 us -> 48.2 us
    pallas_call x1, Pallas kernels: 48.8 us -> 48.2 us  [on_device(): pl.pallas_call(kernel, out_shape=tuple((pltpu.VMEM(o.shape, o.dtype) for...]
where the time goes in v3:
time: 53.9 us; the launch traced here: 53.7 us
  Pallas kernels  48.2 us (89%)
  local copies, waits for them, and re-layouts  4.84 us (9%)
  between operations  0.65 us (1%)
    pallas_call x1, Pallas kernels, on_device(): pl.pallas_call(kernel, out_shape=tuple((pltpu.VMEM(o.shape, o.dtype) for...  48.2 us
    unnamed x6, local copies, waits for them, and re-layouts  4.84 us

profile of v3, /device:TPU:0, one launch (start us, length us, event | category | flops | bytes accessed | tf_op | source)
XLA Modules:
  0.0 53.7 jit_solution(16595087174632668613)
XLA Ops:
  0.6 48.2 %grouped.1 = (bf16[128,4096]{1,0:T(8,128)(2,1)S(1)}, bf16[128,4096]{1,0:T(8,128)(2,1)S(1)}, bf16[128,512]{1,0:T(8,128)(2,1)S(1)}, bf16[128,512]{1,0:T(8,128)(2,1...) custom-call(s32[4]{0:T(128)} %plen_ref.1, s32[4]{0:T(128)} %owner_ref.1, s32[2]{0:T(128)} %rprompt_ref.1, ...), custom_call_target="tpu_custom_call" | custom-call | flops 7000000000 | bytes 7000000 | tf_op jit(solution)/shard_map/grouped/pallas_call | solution.py:250
  48.9 1.0 %copy.22 = bf16[128,4096]{1,0:T(8,128)(2,1)} copy(bf16[128,4096]{1,0:T(8,128)(2,1)S(1)} %get-tuple-element.6) | data formatting | bytes 2097152
  49.9 0.7 %copy.24 = bf16[128,512]{1,0:T(8,128)(2,1)} copy(bf16[128,512]{1,0:T(8,128)(2,1)S(1)} %get-tuple-element.8) | data formatting | bytes 262144
  50.5 0.7 %copy.25 = bf16[128,512]{1,0:T(8,128)(2,1)} copy(bf16[128,512]{1,0:T(8,128)(2,1)S(1)} %get-tuple-element.9) | data formatting | bytes 262144
  51.2 0.8 %copy.26 = f32[256,512]{1,0:T(8,128)} copy(f32[256,512]{1,0:T(8,128)S(1)} %get-tuple-element.10) | data formatting | bytes 1048576
  52.0 0.8 %copy.27 = f32[256,512]{1,0:T(8,128)} copy(f32[256,512]{1,0:T(8,128)S(1)} %get-tuple-element.11) | data formatting | bytes 1048576
  52.8 1.0 %copy.23 = bf16[128,4096]{1,0:T(8,128)(2,1)} copy(bf16[128,4096]{1,0:T(8,128)(2,1)S(1)} %get-tuple-element.7) | data formatting | bytes 2097152
